TPU v7x, 512 devices: a whole 4x8x8 slice. The times are simulated.
512 devices in a mesh: seq: 16 (over x_hi, y), group: 32 (over z, x_lo, core).
Axes of the slice: x: 4 (x_hi: 2, x_lo: 2; x = x_hi * 2 + x_lo), y: 8, z: 8, core: 2. Of those that a mesh axis runs over, the one named last changes fastest.
Arguments:
- query_proj: bfloat16 [32, 1024, 8192], P('group', 'seq'), may hold values from -6 to 6
- key_proj: bfloat16 [32, 1024, 1024], P('group', 'seq'), may hold values from -6 to 6
- value_proj: bfloat16 [32, 1024, 1024], P('group', 'seq'), may hold values from -6 to 6
- query_gain: float32 [128], replicated, may hold values from 1 to 5.5, as said below
- key_gain: float32 [128], replicated, may hold values from 1 to 5.5, as said below
- doc_lengths: int32 [32, 4], P('group'), may hold values from 1 to 512, 1024 in all within a row
Outputs:
- attended: bfloat16 [32, 1024, 8192], P('group', 'seq')
- cache: bfloat16 [16, 32, 32, 1, 16, 256], P('seq', 'group')
Inputs may be any that keep to these rules, and one draw needn't show every extreme that they name: `query_gain`: a gain for each of the 128 features. `key_gain`: a gain for each of the 128 features.
All inputs are finite; a program needn't handle non-finite values.
Results may differ from a plain program's by a relative error of at most 0.0045.
The roundings to bfloat16 on the way count: a program that leaves them out, or rounds other values in their place, can miss the bound.
Values may be sent and summed in bfloat16 or wider, within the bound.
No kernel may reach another device: no remote copies, remote signals or barrier semaphores. Data moves between devices by JAX's collectives and lax.ppermute only.
A program may use at most 64 MiB of HBM per device.

v0:
```python
import math
import jax
import jax.numpy as jnp
from jax import lax
from jax.sharding import PartitionSpec as P

PAGE = 16
NORM_EPS = 1e-06
ROPE_BASE = 1000000.0
MASKED = -1e30


def token_starts(lengths, count):
    doc_ends = jnp.cumsum(lengths)
    token_index = jnp.arange(count, dtype=jnp.int32)
    passed = (doc_ends[None, :] <= token_index[:, None]).astype(jnp.int32)
    return jnp.sum(passed * lengths[None, :], axis=1)


def rope_tables(positions, head_width):
    half_width = head_width // 2
    exponent = jnp.arange(half_width, dtype=jnp.float32) * (-2.0 / head_width)
    inverse = jnp.power(jnp.float32(ROPE_BASE), exponent)
    angles = positions.astype(jnp.float32)[:, None] * inverse[None, :]
    return (jnp.cos(angles), jnp.sin(angles))


def norm_rope(heads_in, gain, cosine, sine):
    values_f = heads_in.astype(jnp.float32)
    inv_rms = lax.rsqrt(jnp.mean(values_f * values_f, axis=-1, keepdims=True) + NORM_EPS)
    normed = values_f * inv_rms * gain
    half_width = heads_in.shape[-1] // 2
    front = normed[..., :half_width]
    back_half = normed[..., half_width:]
    cos_b = cosine[:, None, :]
    sin_b = sine[:, None, :]
    rotated = jnp.concatenate(
        [front * cos_b - back_half * sin_b, back_half * cos_b + front * sin_b], axis=-1
    )
    return rotated.astype(jnp.bfloat16)


def attend(q_all, kv_all, starts, head_width):
    token_count = q_all.shape[0]
    entry_count = q_all.shape[1]
    head_count = q_all.shape[2]
    block_size = math.gcd(token_count, 512)
    block_count = token_count // block_size
    score_scale = 1.0 / math.sqrt(head_width)
    block_range = jnp.arange(block_size, dtype=jnp.int32)

    def one_block(block_id):
        q_first = block_id * block_size
        q_block = lax.dynamic_slice_in_dim(q_all, q_first, block_size, 0)
        q_index = q_first + block_range
        q_start = lax.dynamic_slice_in_dim(starts, q_first, block_size, 0)

        def key_step(key_block, carry):
            run_top, denom, accum = carry
            kv_block = lax.dynamic_slice_in_dim(kv_all, key_block * block_size, block_size, 0)
            k_index = key_block * block_size + block_range
            scores = (
                jnp.einsum(
                    "qend,ked->enqk",
                    q_block,
                    kv_block[..., :head_width],
                    preferred_element_type=jnp.float32,
                )
                * score_scale
            )
            visible = (k_index[None, :] <= q_index[:, None]) & (
                k_index[None, :] >= q_start[:, None]
            )
            scores = jnp.where(visible, scores, MASKED)
            new_top = jnp.maximum(run_top, jnp.max(scores, axis=-1))
            factor = jnp.exp(run_top - new_top)
            weights = jnp.where(visible, jnp.exp(scores - new_top[..., None]), 0.0)
            denom = denom * factor + jnp.sum(weights, axis=-1)
            update = jnp.einsum(
                "enqk,ked->enqd",
                weights.astype(jnp.bfloat16),
                kv_block[..., head_width:],
                preferred_element_type=jnp.float32,
            )
            accum = accum * factor[..., None] + update
            return (new_top, denom, accum)

        start_top = jnp.full((entry_count, head_count, block_size), MASKED, jnp.float32)
        start_sum = jnp.zeros((entry_count, head_count, block_size), jnp.float32)
        start_acc = jnp.zeros((entry_count, head_count, block_size, head_width), jnp.float32)
        run_top, denom, accum = lax.fori_loop(
            0, block_id + 1, key_step, (start_top, start_sum, start_acc)
        )
        return (accum / denom[..., None]).astype(jnp.bfloat16).transpose(2, 0, 1, 3)

    blocks = lax.map(one_block, jnp.arange(block_count, dtype=jnp.int32))
    return blocks.reshape(token_count, entry_count, head_count, head_width)


def page_cache(kv_all, entry_first, repeat):
    token_count, entry_count, pair_width = kv_all.shape
    slots = lax.axis_size("group")
    pages = token_count // (PAGE * repeat * slots)
    paged = kv_all.reshape(pages, repeat, slots, PAGE, entry_count, pair_width)
    copy_class = (entry_first + 0) % repeat
    chosen = lax.dynamic_index_in_dim(paged, copy_class, 1, False)
    picked = [chosen[:, :, :, 0, :]]
    outgoing = jnp.stack(picked)[:, None]
    moved = lax.all_to_all(outgoing, "group", split_axis=3, concat_axis=1, tiled=True)
    return moved.reshape(entry_count, 1, slots, pages, PAGE, pair_width)


def body(query_proj, key_proj, value_proj, query_gain, key_gain, doc_lengths):
    seq_count = lax.axis_size("seq")
    head_width = query_gain.shape[0]
    row_count = query_proj.shape[1]
    q_heads = query_proj.shape[2] // head_width
    kv_heads = key_proj.shape[2] // head_width
    token_count = row_count * seq_count
    entries = max(kv_heads, seq_count)
    repeat = entries // kv_heads
    local_entries = entries // seq_count
    sharing = q_heads // entries
    starts = token_starts(doc_lengths[0], token_count)
    first_row = lax.axis_index("seq") * row_count
    own_index = first_row + jnp.arange(row_count, dtype=jnp.int32)
    own_starts = lax.dynamic_slice_in_dim(starts, first_row, row_count, 0)
    cosine, sine = rope_tables(own_index - own_starts, head_width)
    q_rot = norm_rope(
        query_proj[0].reshape(row_count, q_heads, head_width), query_gain, cosine, sine
    )
    k_rot = norm_rope(key_proj[0].reshape(row_count, kv_heads, head_width), key_gain, cosine, sine)
    pairs = jnp.concatenate(
        [k_rot, value_proj[0].reshape(row_count, kv_heads, head_width)], axis=-1
    )
    spread = jnp.repeat(pairs, repeat, axis=1).reshape(
        row_count, seq_count, local_entries, 2 * head_width
    )
    q_split = q_rot.reshape(row_count, seq_count, local_entries, sharing, head_width)
    entry_first = lax.axis_index("seq") * local_entries
    q_got, kv_got = (
        lax.all_to_all(q_split, "seq", split_axis=1, concat_axis=0, tiled=True),
        lax.all_to_all(spread, "seq", split_axis=1, concat_axis=0, tiled=True),
    )
    q_all = q_got.reshape(token_count, local_entries, sharing, head_width)
    kv_all = kv_got.reshape(token_count, local_entries, 2 * head_width)
    mixed = attend(q_all, kv_all, starts, head_width)
    back = lax.all_to_all(
        mixed.reshape(token_count, 1, local_entries, sharing, head_width),
        "seq",
        split_axis=0,
        concat_axis=1,
        tiled=True,
    )
    cache = page_cache(kv_all, entry_first, repeat)
    attended = back.reshape(1, row_count, q_heads * head_width)
    return (attended, cache)


def solution(mesh):
    in_specs = (
        P("group", "seq", None),
        P("group", "seq", None),
        P("group", "seq", None),
        P(),
        P(),
        P("group", None),
    )
    out_specs = (P("group", "seq", None), P("seq", "group", None, None, None, None))
    return jax.shard_map(body, mesh=mesh, in_specs=in_specs, out_specs=out_specs, check_vma=False)
```

profile of v0, /device:TPU:2, one launch (start us, length us, event | category | flops | bytes accessed | tf_op | source)
XLA Modules:
  0.0 150.2 jit_solution(15361947048695826945)
XLA Ops:
  0.7 0.9 reduce-window.8
  1.6 0.9 convert_bitcast_fusion.1
  2.9 0.9 copy.72
  6.0 0.9 broadcast_in_dim.18
  6.8 8.8 %all-to-all-start.1 = ((bf16[64,16,1,256]{3,0,2,1:T(8,128)(2,1)}), bf16[64,16,1,256]{3,0,2,1:T(8,128)(2,1)S(1)}, u32[]{:S(2)}, u32[]{:S(2)}) async-start(bf16[64,16,1,256]{3,0,2,1:T(8,128)(2,1)} %bitcast.22), calls=%async_computation.1 | async-start | bytes 1048576 | tf_op jit(solution)/shard_map/all_to_all | solution.py:143
  16.8 0.9 multiply_multiply_fusion
  17.7 0.9 subtract_convert_fusion
  20.0 1.6 %maximum_bitcast_fusion = bf16[64,16,1,4,128]{4,0,3,2,1:T(8,128)(2,1)} fusion(bf16[64,16,1,4,64]{4,0,3,1,2:T(8,128)(2,1)S(1)} %bitcast.144, bf16[64,16,1,4,64]{4,0,3,1,2:T(8,128)(2,1)S(1)} %bitcast.143), kind=kLoop, calls=%fused_computation.35 | loop fusion | flops 2097152 | bytes 2097152 | tf_op jit(solution)/shard_map/concatenate | solution.py:37
  21.6 11.3 %all-to-all-done.1 = bf16[64,16,1,256]{3,0,2,1:T(8,128)(2,1)S(1)} async-done(((bf16[64,16,1,256]{3,0,2,1:T(8,128)(2,1)}), bf16[64,16,1,256]{3,0,2,1:T(8,128)(2,1)S(1)}, u32[]{:S(2)}, u32[]{:S(2)}) %all-to-all-start.1) | async-done | bytes 524320 | tf_op jit(solution)/shard_map/all_to_all | solution.py:143
  32.8 4.5 %all-to-all-start = ((bf16[64,16,1,4,128]{4,0,3,2,1:T(8,128)(2,1)}), bf16[64,16,1,4,128]{4,0,3,2,1:T(8,128)(2,1)S(1)}, u32[]{:S(2)}, u32[]{:S(2)}) async-start(bf16[64,16,1,4,128]{4,0,3,2,1:T(8,128)(2,1)} %maximum_bitcast_fusion), calls=%async_computation | async-start | bytes 2097152 | tf_op jit(solution)/shard_map/all_to_all | solution.py:142
  38.1 26.5 %all-to-all-done = bf16[64,16,1,4,128]{4,0,3,2,1:T(8,128)(2,1)S(1)} async-done(((bf16[64,16,1,4,128]{4,0,3,2,1:T(8,128)(2,1)}), bf16[64,16,1,4,128]{4,0,3,2,1:T(8,128)(2,1)S(1)}, u32[]{:S(2)}, u32[]{:S(2)}) %all-to-all-start) | async-done | bytes 1048608 | tf_op jit(solution)/shard_map/all_to_all | solution.py:142
  64.6 12.0 %all-to-all-start.3 = ((bf16[1,1,1,32,16,256]{5,4,2,1,0,3:T(8,128)(2,1)}), bf16[1,1,1,32,16,256]{5,4,2,1,0,3:T(8,128)(2,1)}, u32[]{:S(2)}, u32[]{:S(2)}) async-start(bf16[1,1,1,32,16,256]{5,4,2,1,0,3:T(8,128)(2,1)} %dynamic-slice_bitcast_fusion.4), calls=%async_computation.3 | async-start | bytes 524288 | tf_op jit(solution)/shard_map/all_to_all | solution.py:109
  76.7 32.0 %while.29 = (s32[]{:T(128)}, bf16[2,512,1,4,128]{4,1,0,3,2:T(8,128)(2,1)}, s32[2]{0:T(128)S(1)}, bf16[1024,1,4,128]{3,0,2,1:T(8,128)(2,1)S(1)}, s32[1024]{0:T(10...) while((s32[]{:T(128)}, ...), condition=%wide.region_9.10_spmd.clone.clone, body=%wide.region_4.9_spmd.clone.clone.sunk | while | flops 552344576 | bytes 37137528 | solution.py:96
  78.8 8.5 %while.30 = (s32[]{:T(128)}, f32[1,4,512]{2,1,0:T(4,128)S(1)}, f32[1,4,512]{2,1,0:T(4,128)S(1)}, f32[1,4,512,128]{3,2,1,0:T(8,128)S(1)}, s32[]{:T(128)}, /*index...) while((s32[]{:T(128)}, f32[1,4,512]{2,1,0:T(4,128)S(1)}, ...), condition=%wide.region_8.8_spmd, body=%wide.region_5.7_spmd.sunk | while | flops 551819776 | bytes 33433844 | solution.py:91
  79.2 2.8 %fusion.29 = (f32[4,512]{1,0:T(4,128)S(1)}, f32[512,512,4]{1,0,2:T(8,128)}) fusion(pred[512,512]{0,1:T(8,128)(4,1)S(1)} %compare_and_fusion.2, bf16[512,1,4,128]{3,0,2,1:T(8,128)(2,1)S(1)} %get-tuple-element.354, bf16[1024,1,256]{2,0,1:T(8,128)(2,1)S(1)} %get-tuple-element.353, s32[]{:T(128)S(6)} %select_n.74), kind=kOutput, calls=%fused_computation.3.clone.1 | convolution fusion | flops 271579136 | bytes 5120004 | tf_op jit(solution)/shard_map/while/body/eval_jaxpr/while/body/qend,ked->enqk/dot_general | solution.py:63
  82.0 4.2 %fusion.32 = f32[1,4,512,128]{3,2,1,0:T(8,128)S(1)} fusion(f32[512,512,4]{1,0,2:T(8,128)} %get-tuple-element.313, f32[4,512]{1,0:T(4,128)S(1)} %bitcast.136, pred[512,512]{0,1:T(8,128)(4,1)S(1)} %compare_and_fusion.2, f32[1,4,512,128]{3,2,1,0:T(8,128)S(1)} %get-tuple-element.333, f32[4,512]{1,0:T(4,128)S(1)} %get-tuple-element.314, ...), kind=kOutput, calls=%fused_computation.10.clone.1 | convolution fusion | flops 274202624 | bytes 6701064 | tf_op jit(solution)/shard_map/while/body/eval_jaxpr/while/body/enqk,ked->enqd/dot_general | solution.py:79
  86.2 1.0 fusion.31
  87.3 1.1 bitcast_dynamic-update-slice_fusion.2
  90.6 16.9 %while.30 = (s32[]{:T(128)}, f32[1,4,512]{2,1,0:T(4,128)S(1)}, f32[1,4,512]{2,1,0:T(4,128)S(1)}, f32[1,4,512,128]{3,2,1,0:T(8,128)S(1)}, s32[]{:T(128)}, /*index...) while((s32[]{:T(128)}, f32[1,4,512]{2,1,0:T(4,128)S(1)}, ...), condition=%wide.region_8.8_spmd, body=%wide.region_5.7_spmd.sunk | while | flops 551819776 | bytes 33433844 | solution.py:91
  90.9 2.8 %fusion.29 = (f32[4,512]{1,0:T(4,128)S(1)}, f32[512,512,4]{1,0,2:T(8,128)}) fusion(pred[512,512]{0,1:T(8,128)(4,1)S(1)} %compare_and_fusion.2, bf16[512,1,4,128]{3,0,2,1:T(8,128)(2,1)S(1)} %get-tuple-element.354, bf16[1024,1,256]{2,0,1:T(8,128)(2,1)S(1)} %get-tuple-element.353, s32[]{:T(128)S(6)} %select_n.74), kind=kOutput, calls=%fused_computation.3.clone.1 | convolution fusion | flops 271579136 | bytes 5120004 | tf_op jit(solution)/shard_map/while/body/eval_jaxpr/while/body/qend,ked->enqk/dot_general | solution.py:63
  93.8 4.2 %fusion.32 = f32[1,4,512,128]{3,2,1,0:T(8,128)S(1)} fusion(f32[512,512,4]{1,0,2:T(8,128)} %get-tuple-element.313, f32[4,512]{1,0:T(4,128)S(1)} %bitcast.136, pred[512,512]{0,1:T(8,128)(4,1)S(1)} %compare_and_fusion.2, f32[1,4,512,128]{3,2,1,0:T(8,128)S(1)} %get-tuple-element.333, f32[4,512]{1,0:T(4,128)S(1)} %get-tuple-element.314, ...), kind=kOutput, calls=%fused_computation.10.clone.1 | convolution fusion | flops 274202624 | bytes 6701064 | tf_op jit(solution)/shard_map/while/body/eval_jaxpr/while/body/enqk,ked->enqd/dot_general | solution.py:79
  98.0 1.0 fusion.31
  99.4 2.8 %fusion.29 = (f32[4,512]{1,0:T(4,128)S(1)}, f32[512,512,4]{1,0,2:T(8,128)}) fusion(pred[512,512]{0,1:T(8,128)(4,1)S(1)} %compare_and_fusion.2, bf16[512,1,4,128]{3,0,2,1:T(8,128)(2,1)S(1)} %get-tuple-element.354, bf16[1024,1,256]{2,0,1:T(8,128)(2,1)S(1)} %get-tuple-element.353, s32[]{:T(128)S(6)} %select_n.74), kind=kOutput, calls=%fused_computation.3.clone.1 | convolution fusion | flops 271579136 | bytes 5120004 | tf_op jit(solution)/shard_map/while/body/eval_jaxpr/while/body/qend,ked->enqk/dot_general | solution.py:63
  102.2 4.2 %fusion.32 = f32[1,4,512,128]{3,2,1,0:T(8,128)S(1)} fusion(f32[512,512,4]{1,0,2:T(8,128)} %get-tuple-element.313, f32[4,512]{1,0:T(4,128)S(1)} %bitcast.136, pred[512,512]{0,1:T(8,128)(4,1)S(1)} %compare_and_fusion.2, f32[1,4,512,128]{3,2,1,0:T(8,128)S(1)} %get-tuple-element.333, f32[4,512]{1,0:T(4,128)S(1)} %get-tuple-element.314, ...), kind=kOutput, calls=%fused_computation.10.clone.1 | convolution fusion | flops 274202624 | bytes 6701064 | tf_op jit(solution)/shard_map/while/body/eval_jaxpr/while/body/enqk,ked->enqd/dot_general | solution.py:79
  106.5 1.0 fusion.31
  107.6 1.1 bitcast_dynamic-update-slice_fusion.2
  108.7 3.0 %copy.63 = bf16[1024,1,1,4,128]{4,3,2,1,0:T(4,128)(2,1)} copy(bf16[1024,1,1,4,128]{4,0,3,2,1:T(8,128)(2,1)} %bitcast.147) | data formatting | bytes 2097152 | tf_op jit(solution)/shard_map/reshape;reshape | solution.py:149
  111.7 5.2 %all-to-all-start.2 = ((bf16[1024,1,1,4,128]{4,3,2,1,0:T(4,128)(2,1)}), bf16[1024,1,1,4,128]{4,3,2,1,0:T(4,128)(2,1)S(1)}, u32[]{:S(2)}, u32[]{:S(2)}) async-start(bf16[1024,1,1,4,128]{4,3,2,1,0:T(4,128)(2,1)} %copy.63), calls=%async_computation.2 | async-start | bytes 2097152 | tf_op jit(solution)/shard_map/all_to_all | solution.py:148
  117.0 28.9 %all-to-all-done.2 = bf16[1024,1,1,4,128]{4,3,2,1,0:T(4,128)(2,1)S(1)} async-done(((bf16[1024,1,1,4,128]{4,3,2,1,0:T(4,128)(2,1)}), bf16[1024,1,1,4,128]{4,3,2,1,0:T(4,128)(2,1)S(1)}, u32[]{:S(2)}, u32[]{:S(2)}) %all-to-all-start.2) | async-done | bytes 1048608 | tf_op jit(solution)/shard_map/all_to_all | solution.py:148
  146.1 0.8 copy.65
  146.9 1.6 %reshape.193 = bf16[1,64,8192]{2,1,0:T(8,128)(2,1)} reshape(bf16[64,16,1,1,4,128]{5,4,1,0,3,2:T(4,128)(2,1)S(1)} %copy.65) | data formatting | bytes 2097152 | tf_op jit(solution)/shard_map/reshape | solution.py:156
  148.5 1.7 %copy.95 = bf16[1,1,32,1,16,256]{5,4,3,2,1,0:T(8,128)(2,1)} copy(bf16[1,1,32,1,16,256]{5,4,3,2,1,0:T(8,128)(2,1)} %bitcast.33) | data formatting | bytes 524288
  (66 shorter events, 8.6 us)
Async XLA Ops:
  0.6 15.0 %copy-start.1 = (bf16[1,64,8192]{2,1,0:T(8,128)(2,1)S(1)}, bf16[1,64,8192]{2,1,0:T(8,128)(2,1)}, u32[]{:S(2)}) copy-start(bf16[1,64,8192]{2,1,0:T(8,128)(2,1)} %param.10) | copy-start | bytes 3145732
  6.8 26.0 %all-to-all-start.1 = ((bf16[64,16,1,256]{3,0,2,1:T(8,128)(2,1)}), bf16[64,16,1,256]{3,0,2,1:T(8,128)(2,1)S(1)}, u32[]{:S(2)}, u32[]{:S(2)}) async-start(bf16[64,16,1,256]{3,0,2,1:T(8,128)(2,1)} %bitcast.22), calls=%async_computation.1 | async-start | bytes 1048576 | tf_op jit(solution)/shard_map/all_to_all | solution.py:143
  15.6 1.2 copy-start.2
  32.8 31.8 %all-to-all-start = ((bf16[64,16,1,4,128]{4,0,3,2,1:T(8,128)(2,1)}), bf16[64,16,1,4,128]{4,0,3,2,1:T(8,128)(2,1)S(1)}, u32[]{:S(2)}, u32[]{:S(2)}) async-start(bf16[64,16,1,4,128]{4,0,3,2,1:T(8,128)(2,1)} %maximum_bitcast_fusion), calls=%async_computation | async-start | bytes 2097152 | tf_op jit(solution)/shard_map/all_to_all | solution.py:142
  64.6 47.2 %all-to-all-start.3 = ((bf16[1,1,1,32,16,256]{5,4,2,1,0,3:T(8,128)(2,1)}), bf16[1,1,1,32,16,256]{5,4,2,1,0,3:T(8,128)(2,1)}, u32[]{:S(2)}, u32[]{:S(2)}) async-start(bf16[1,1,1,32,16,256]{5,4,2,1,0,3:T(8,128)(2,1)} %dynamic-slice_bitcast_fusion.4), calls=%async_computation.3 | async-start | bytes 524288 | tf_op jit(solution)/shard_map/all_to_all | solution.py:109
  82.0 4.3 %copy-start = (f32[512,512,4]{1,0,2:T(8,128)S(1)}, f32[512,512,4]{1,0,2:T(8,128)}, u32[]{:S(2)}) copy-start(f32[512,512,4]{1,0,2:T(8,128)} %get-tuple-element.313) | copy-start | bytes 12582916 | tf_op jit(solution)/shard_map/while/body/eval_jaxpr/while
  93.7 4.3 %copy-start = (f32[512,512,4]{1,0,2:T(8,128)S(1)}, f32[512,512,4]{1,0,2:T(8,128)}, u32[]{:S(2)}) copy-start(f32[512,512,4]{1,0,2:T(8,128)} %get-tuple-element.313) | copy-start | bytes 12582916 | tf_op jit(solution)/shard_map/while/body/eval_jaxpr/while
  102.2 4.3 %copy-start = (f32[512,512,4]{1,0,2:T(8,128)S(1)}, f32[512,512,4]{1,0,2:T(8,128)}, u32[]{:S(2)}) copy-start(f32[512,512,4]{1,0,2:T(8,128)} %get-tuple-element.313) | copy-start | bytes 12582916 | tf_op jit(solution)/shard_map/while/body/eval_jaxpr/while
  111.7 34.2 %all-to-all-start.2 = ((bf16[1024,1,1,4,128]{4,3,2,1,0:T(4,128)(2,1)}), bf16[1024,1,1,4,128]{4,3,2,1,0:T(4,128)(2,1)S(1)}, u32[]{:S(2)}, u32[]{:S(2)}) async-start(bf16[1024,1,1,4,128]{4,3,2,1,0:T(4,128)(2,1)} %copy.63), calls=%async_computation.2 | async-start | bytes 2097152 | tf_op jit(solution)/shard_map/all_to_all | solution.py:148
where the time goes:
time: 151 us; the launch traced here: 150 us
  waiting for transfers between devices  66.7 us (44%)
  starting transfers between devices  30.6 us (20%)
  matrix products  21.1 us (14%)
  other arithmetic  14.6 us (10%)
  local copies, waits for them, and re-layouts  13.5 us (9%)
  loops' own time  2.91 us (2%)
    all_to_all x1, waiting for transfers between devices, body(): lax.all_to_all(mixed.reshape(token_count, 1, local_entries, sharing, head...  28.9 us
    all_to_all x1, waiting for transfers between devices, body(): lax.all_to_all(q_split, 'seq', split_axis=1, concat_axis=0, tiled=True)  26.5 us
    dot_general x3, matrix products, key_step(): jnp.einsum('enqk,ked->enqd', weights.astype(jnp.bfloat16), kv_block[...,...  12.7 us
    all_to_all x1, starting transfers between devices, page_cache(): lax.all_to_all(outgoing, 'group', split_axis=3, concat_axis=1, tiled=True)  12 us
    all_to_all x1, waiting for transfers between devices, body(): lax.all_to_all(spread, 'seq', split_axis=1, concat_axis=0, tiled=True)  11.3 us
    all_to_all x1, starting transfers between devices, body(): lax.all_to_all(spread, 'seq', split_axis=1, concat_axis=0, tiled=True)  8.77 us
    dot_general x3, matrix products, key_step(): jnp.einsum('qend,ked->enqk', q_block, kv_block[..., :head_width], preferr...  8.42 us
    all_to_all x1, starting transfers between devices, body(): lax.all_to_all(mixed.reshape(token_count, 1, local_entries, sharing, head...  5.24 us
  transfers between devices with their start and end apart: 4, of which 3 were waited for; matrix products, arithmetic and copies ran while one was open for 26% of the time, Pallas kernels for 0%

commit v1 on v0

--- a/solution.py
+++ b/solution.py
@@ -145,12 +145,20 @@
     q_all = q_got.reshape(token_count, local_entries, sharing, head_width)
     kv_all = kv_got.reshape(token_count, local_entries, 2 * head_width)
     mixed = attend(q_all, kv_all, starts, head_width)
-    back = lax.all_to_all(
-        mixed.reshape(token_count, 1, local_entries, sharing, head_width),
-        "seq",
-        split_axis=0,
-        concat_axis=1,
-        tiled=True,
+    back = jnp.concatenate(
+        lax.all_to_all(
+            jnp.stack(
+                jnp.split(
+                    mixed.reshape(token_count, 1, local_entries, sharing, head_width),
+                    lax.axis_size("seq"),
+                    axis=0,
+                )
+            ),
+            "seq",
+            0,
+            0,
+        ),
+        axis=1,
     )
     cache = page_cache(kv_all, entry_first, repeat)
     attended = back.reshape(1, row_count, q_heads * head_width)

time: 151 us -> 172 us (1.14)
  local copies, waits for them, and re-layouts: 13.5 us -> 33.9 us
    unnamed x8 -> x23, local copies, waits for them, and re-layouts: 3.04 us -> 25.1 us
    another operation x9 -> x10, local copies, waits for them, and re-layouts: 4.53 us -> 4.6 us  [the longest x1 1.61 us: body(): attended = back.reshape(1, row_count, q_heads * head_width)]
  transfers between devices with their start and end apart: 4 -> 4, of which waited for: 3 -> 3; matrix products, arithmetic and copies ran while one was open for 26% -> 35% of each run, Pallas kernels for 0% -> 0%
where the time goes in v1:
time: 172 us; the launch traced here: 171 us
  waiting for transfers between devices  66.7 us (39%)
  local copies, waits for them, and re-layouts  33.9 us (20%)
  starting transfers between devices  30.5 us (18%)
  matrix products  21.1 us (12%)
  other arithmetic  14.6 us (8%)
  loops' own time  2.91 us (2%)
    all_to_all x1, waiting for transfers between devices, body(): lax.all_to_all(jnp.stack(jnp.split(mixed.reshape(token_count, 1, local_en...  28.9 us
    all_to_all x1, waiting for transfers between devices, body(): lax.all_to_all(q_split, 'seq', split_axis=1, concat_axis=0, tiled=True)  26.5 us
    unnamed x23, local copies, waits for them, and re-layouts  25.1 us
    dot_general x3, matrix products, key_step(): jnp.einsum('enqk,ked->enqd', weights.astype(jnp.bfloat16), kv_block[...,...  12.7 us
    all_to_all x1, starting transfers between devices, page_cache(): lax.all_to_all(outgoing, 'group', split_axis=3, concat_axis=1, tiled=True)  12 us
    all_to_all x1, waiting for transfers between devices, body(): lax.all_to_all(spread, 'seq', split_axis=1, concat_axis=0, tiled=True)  11.3 us
    all_to_all x1, starting transfers between devices, body(): lax.all_to_all(spread, 'seq', split_axis=1, concat_axis=0, tiled=True)  8.77 us
    dot_general x3, matrix products, key_step(): jnp.einsum('qend,ked->enqk', q_block, kv_block[..., :head_width], preferr...  8.43 us
  transfers between devices with their start and end apart: 4, of which 3 were waited for; matrix products, arithmetic and copies ran while one was open for 35% of the time, Pallas kernels for 0%

profile of v1, /device:TPU:2, one launch (start us, length us, event | category | flops | bytes accessed | tf_op | source)
XLA Modules:
  0.0 170.5 jit_solution(2355273898970478362)
XLA Ops:
  6.8 8.8 %all-to-all-start.1 = ((bf16[64,16,1,256]{3,0,2,1:T(8,128)(2,1)}), bf16[64,16,1,256]{3,0,2,1:T(8,128)(2,1)S(1)}, u32[]{:S(2)}, u32[]{:S(2)}) async-start(bf16[64,16,1,256]{3,0,2,1:T(8,128)(2,1)} %bitcast.22), calls=%async_computation.1 | async-start | bytes 1048576 | tf_op jit(solution)/shard_map/all_to_all | solution.py:143
  20.0 1.6 maximum_bitcast_fusion
  21.6 11.3 %all-to-all-done.1 = bf16[64,16,1,256]{3,0,2,1:T(8,128)(2,1)S(1)} async-done(((bf16[64,16,1,256]{3,0,2,1:T(8,128)(2,1)}), bf16[64,16,1,256]{3,0,2,1:T(8,128)(2,1)S(1)}, u32[]{:S(2)}, u32[]{:S(2)}) %all-to-all-start.1) | async-done | bytes 524320 | tf_op jit(solution)/shard_map/all_to_all | solution.py:143
  32.8 4.5 %all-to-all-start = ((bf16[64,16,1,4,128]{4,0,3,2,1:T(8,128)(2,1)}), bf16[64,16,1,4,128]{4,0,3,2,1:T(8,128)(2,1)S(1)}, u32[]{:S(2)}, u32[]{:S(2)}) async-start(bf16[64,16,1,4,128]{4,0,3,2,1:T(8,128)(2,1)} %maximum_bitcast_fusion), calls=%async_computation | async-start | bytes 2097152 | tf_op jit(solution)/shard_map/all_to_all | solution.py:142
  38.1 26.5 %all-to-all-done = bf16[64,16,1,4,128]{4,0,3,2,1:T(8,128)(2,1)S(1)} async-done(((bf16[64,16,1,4,128]{4,0,3,2,1:T(8,128)(2,1)}), bf16[64,16,1,4,128]{4,0,3,2,1:T(8,128)(2,1)S(1)}, u32[]{:S(2)}, u32[]{:S(2)}) %all-to-all-start) | async-done | bytes 1048608 | tf_op jit(solution)/shard_map/all_to_all | solution.py:142
  64.6 12.0 %all-to-all-start.3 = ((bf16[1,1,1,32,16,256]{5,4,2,1,0,3:T(8,128)(2,1)}), bf16[1,1,1,32,16,256]{5,4,2,1,0,3:T(8,128)(2,1)}, u32[]{:S(2)}, u32[]{:S(2)}) async-start(bf16[1,1,1,32,16,256]{5,4,2,1,0,3:T(8,128)(2,1)} %dynamic-slice_bitcast_fusion.4), calls=%async_computation.3 | async-start | bytes 524288 | tf_op jit(solution)/shard_map/all_to_all | solution.py:109
  76.7 32.0 %while.29 = (s32[]{:T(128)}, bf16[2,512,1,4,128]{4,1,0,3,2:T(8,128)(2,1)}, s32[2]{0:T(128)S(1)}, bf16[1024,1,4,128]{3,0,2,1:T(8,128)(2,1)S(1)}, s32[1024]{0:T(10...) while((s32[]{:T(128)}, ...), condition=%wide.region_9.10_spmd.clone.clone, body=%wide.region_4.9_spmd.clone.clone.sunk | while | flops 552344576 | bytes 37137528 | solution.py:96
  78.8 8.5 %while.30 = (s32[]{:T(128)}, f32[1,4,512]{2,1,0:T(4,128)S(1)}, f32[1,4,512]{2,1,0:T(4,128)S(1)}, f32[1,4,512,128]{3,2,1,0:T(8,128)S(1)}, s32[]{:T(128)}, /*index...) while((s32[]{:T(128)}, f32[1,4,512]{2,1,0:T(4,128)S(1)}, ...), condition=%wide.region_8.8_spmd, body=%wide.region_5.7_spmd.sunk | while | flops 551819776 | bytes 33433844 | solution.py:91
  79.2 2.8 %fusion.45 = (f32[4,512]{1,0:T(4,128)S(1)}, f32[512,512,4]{1,0,2:T(8,128)}) fusion(pred[512,512]{0,1:T(8,128)(4,1)S(1)} %compare_and_fusion.2, bf16[512,1,4,128]{3,0,2,1:T(8,128)(2,1)S(1)} %get-tuple-element.354, bf16[1024,1,256]{2,0,1:T(8,128)(2,1)S(1)} %get-tuple-element.353, s32[]{:T(128)S(6)} %select_n.74), kind=kOutput, calls=%fused_computation.3.clone.1 | convolution fusion | flops 271579136 | bytes 5120004 | tf_op jit(solution)/shard_map/while/body/eval_jaxpr/while/body/qend,ked->enqk/dot_general | solution.py:63
  82.0 4.2 %fusion.48 = f32[1,4,512,128]{3,2,1,0:T(8,128)S(1)} fusion(f32[512,512,4]{1,0,2:T(8,128)} %get-tuple-element.313, f32[4,512]{1,0:T(4,128)S(1)} %bitcast.198, pred[512,512]{0,1:T(8,128)(4,1)S(1)} %compare_and_fusion.2, f32[1,4,512,128]{3,2,1,0:T(8,128)S(1)} %get-tuple-element.333, f32[4,512]{1,0:T(4,128)S(1)} %get-tuple-element.314, ...), kind=kOutput, calls=%fused_computation.10.clone.1 | convolution fusion | flops 274202624 | bytes 6701064 | tf_op jit(solution)/shard_map/while/body/eval_jaxpr/while/body/enqk,ked->enqd/dot_general | solution.py:79
  90.6 17.0 %while.30 = (s32[]{:T(128)}, f32[1,4,512]{2,1,0:T(4,128)S(1)}, f32[1,4,512]{2,1,0:T(4,128)S(1)}, f32[1,4,512,128]{3,2,1,0:T(8,128)S(1)}, s32[]{:T(128)}, /*index...) while((s32[]{:T(128)}, f32[1,4,512]{2,1,0:T(4,128)S(1)}, ...), condition=%wide.region_8.8_spmd, body=%wide.region_5.7_spmd.sunk | while | flops 551819776 | bytes 33433844 | solution.py:91
  90.9 2.8 %fusion.45 = (f32[4,512]{1,0:T(4,128)S(1)}, f32[512,512,4]{1,0,2:T(8,128)}) fusion(pred[512,512]{0,1:T(8,128)(4,1)S(1)} %compare_and_fusion.2, bf16[512,1,4,128]{3,0,2,1:T(8,128)(2,1)S(1)} %get-tuple-element.354, bf16[1024,1,256]{2,0,1:T(8,128)(2,1)S(1)} %get-tuple-element.353, s32[]{:T(128)S(6)} %select_n.74), kind=kOutput, calls=%fused_computation.3.clone.1 | convolution fusion | flops 271579136 | bytes 5120004 | tf_op jit(solution)/shard_map/while/body/eval_jaxpr/while/body/qend,ked->enqk/dot_general | solution.py:63
  93.8 4.2 %fusion.48 = f32[1,4,512,128]{3,2,1,0:T(8,128)S(1)} fusion(f32[512,512,4]{1,0,2:T(8,128)} %get-tuple-element.313, f32[4,512]{1,0:T(4,128)S(1)} %bitcast.198, pred[512,512]{0,1:T(8,128)(4,1)S(1)} %compare_and_fusion.2, f32[1,4,512,128]{3,2,1,0:T(8,128)S(1)} %get-tuple-element.333, f32[4,512]{1,0:T(4,128)S(1)} %get-tuple-element.314, ...), kind=kOutput, calls=%fused_computation.10.clone.1 | convolution fusion | flops 274202624 | bytes 6701064 | tf_op jit(solution)/shard_map/while/body/eval_jaxpr/while/body/enqk,ked->enqd/dot_general | solution.py:79
  99.4 2.8 %fusion.45 = (f32[4,512]{1,0:T(4,128)S(1)}, f32[512,512,4]{1,0,2:T(8,128)}) fusion(pred[512,512]{0,1:T(8,128)(4,1)S(1)} %compare_and_fusion.2, bf16[512,1,4,128]{3,0,2,1:T(8,128)(2,1)S(1)} %get-tuple-element.354, bf16[1024,1,256]{2,0,1:T(8,128)(2,1)S(1)} %get-tuple-element.353, s32[]{:T(128)S(6)} %select_n.74), kind=kOutput, calls=%fused_computation.3.clone.1 | convolution fusion | flops 271579136 | bytes 5120004 | tf_op jit(solution)/shard_map/while/body/eval_jaxpr/while/body/qend,ked->enqk/dot_general | solution.py:63
  102.2 4.2 %fusion.48 = f32[1,4,512,128]{3,2,1,0:T(8,128)S(1)} fusion(f32[512,512,4]{1,0,2:T(8,128)} %get-tuple-element.313, f32[4,512]{1,0:T(4,128)S(1)} %bitcast.198, pred[512,512]{0,1:T(8,128)(4,1)S(1)} %compare_and_fusion.2, f32[1,4,512,128]{3,2,1,0:T(8,128)S(1)} %get-tuple-element.333, f32[4,512]{1,0:T(4,128)S(1)} %get-tuple-element.314, ...), kind=kOutput, calls=%fused_computation.10.clone.1 | convolution fusion | flops 274202624 | bytes 6701064 | tf_op jit(solution)/shard_map/while/body/eval_jaxpr/while/body/enqk,ked->enqd/dot_general | solution.py:79
  110.2 1.5 fusion.37
  111.6 1.5 fusion.36
  113.1 1.5 fusion.35
  114.6 1.5 fusion.34
  117.5 1.5 fusion.32
  119.0 1.5 fusion.31
  120.4 1.5 fusion.30
  121.9 1.5 fusion.29
  124.9 1.5 fusion.27
  126.3 1.5 fusion.26
  127.8 1.5 fusion.25
  129.3 1.5 fusion.24
  130.8 1.5 fusion.23
  132.2 5.2 %all-to-all-start.2 = ((bf16[16,64,1,1,4,128]{5,1,4,3,2,0:T(8,128)(2,1)}), bf16[16,64,1,1,4,128]{5,1,4,3,2,0:T(8,128)(2,1)S(1)}, u32[]{:S(2)}, u32[]{:S(2)}) async-start(bf16[16,64,1,1,4,128]{5,1,4,3,2,0:T(8,128)(2,1)} %fusion.23), calls=%async_computation.2 | async-start | bytes 2097152 | tf_op jit(solution)/shard_map/all_to_all | solution.py:149
  137.5 28.9 %all-to-all-done.2 = bf16[16,64,1,1,4,128]{5,1,4,3,2,0:T(8,128)(2,1)S(1)} async-done(((bf16[16,64,1,1,4,128]{5,1,4,3,2,0:T(8,128)(2,1)}), bf16[16,64,1,1,4,128]{5,1,4,3,2,0:T(8,128)(2,1)S(1)}, u32[]{:S(2)}, u32[]{:S(2)}) %all-to-all-start.2) | async-done | bytes 1048608 | tf_op jit(solution)/shard_map/all_to_all | solution.py:149
  167.2 1.6 reshape_reshape.14
  168.8 1.7 copy.117
  (80 shorter events, 24.4 us)
Async XLA Ops:
  0.6 15.0 %copy-start.1 = (bf16[1,64,8192]{2,1,0:T(8,128)(2,1)S(1)}, bf16[1,64,8192]{2,1,0:T(8,128)(2,1)}, u32[]{:S(2)}) copy-start(bf16[1,64,8192]{2,1,0:T(8,128)(2,1)} %param.10) | copy-start | bytes 3145732
  6.8 26.0 %all-to-all-start.1 = ((bf16[64,16,1,256]{3,0,2,1:T(8,128)(2,1)}), bf16[64,16,1,256]{3,0,2,1:T(8,128)(2,1)S(1)}, u32[]{:S(2)}, u32[]{:S(2)}) async-start(bf16[64,16,1,256]{3,0,2,1:T(8,128)(2,1)} %bitcast.22), calls=%async_computation.1 | async-start | bytes 1048576 | tf_op jit(solution)/shard_map/all_to_all | solution.py:143
  15.6 1.2 copy-start.2
  32.8 31.8 %all-to-all-start = ((bf16[64,16,1,4,128]{4,0,3,2,1:T(8,128)(2,1)}), bf16[64,16,1,4,128]{4,0,3,2,1:T(8,128)(2,1)S(1)}, u32[]{:S(2)}, u32[]{:S(2)}) async-start(bf16[64,16,1,4,128]{4,0,3,2,1:T(8,128)(2,1)} %maximum_bitcast_fusion), calls=%async_computation | async-start | bytes 2097152 | tf_op jit(solution)/shard_map/all_to_all | solution.py:142
  64.6 67.6 %all-to-all-start.3 = ((bf16[1,1,1,32,16,256]{5,4,2,1,0,3:T(8,128)(2,1)}), bf16[1,1,1,32,16,256]{5,4,2,1,0,3:T(8,128)(2,1)}, u32[]{:S(2)}, u32[]{:S(2)}) async-start(bf16[1,1,1,32,16,256]{5,4,2,1,0,3:T(8,128)(2,1)} %dynamic-slice_bitcast_fusion.4), calls=%async_computation.3 | async-start | bytes 524288 | tf_op jit(solution)/shard_map/all_to_all | solution.py:109
  82.0 4.3 %copy-start = (f32[512,512,4]{1,0,2:T(8,128)S(1)}, f32[512,512,4]{1,0,2:T(8,128)}, u32[]{:S(2)}) copy-start(f32[512,512,4]{1,0,2:T(8,128)} %get-tuple-element.313) | copy-start | bytes 12582916 | tf_op jit(solution)/shard_map/while/body/eval_jaxpr/while
  93.7 4.3 %copy-start = (f32[512,512,4]{1,0,2:T(8,128)S(1)}, f32[512,512,4]{1,0,2:T(8,128)}, u32[]{:S(2)}) copy-start(f32[512,512,4]{1,0,2:T(8,128)} %get-tuple-element.313) | copy-start | bytes 12582916 | tf_op jit(solution)/shard_map/while/body/eval_jaxpr/while
  102.2 4.3 %copy-start = (f32[512,512,4]{1,0,2:T(8,128)S(1)}, f32[512,512,4]{1,0,2:T(8,128)}, u32[]{:S(2)}) copy-start(f32[512,512,4]{1,0,2:T(8,128)} %get-tuple-element.313) | copy-start | bytes 12582916 | tf_op jit(solution)/shard_map/while/body/eval_jaxpr/while
  132.2 34.2 %all-to-all-start.2 = ((bf16[16,64,1,1,4,128]{5,1,4,3,2,0:T(8,128)(2,1)}), bf16[16,64,1,1,4,128]{5,1,4,3,2,0:T(8,128)(2,1)S(1)}, u32[]{:S(2)}, u32[]{:S(2)}) async-start(bf16[16,64,1,1,4,128]{5,1,4,3,2,0:T(8,128)(2,1)} %fusion.23), calls=%async_computation.2 | async-start | bytes 2097152 | tf_op jit(solution)/shard_map/all_to_all | solution.py:149
